TPU v7x, 512 devices: a whole 4x4x16 slice. The times are simulated.
512 devices in a mesh: stream: 16 (over z_lo, y), cross: 32 (over z_hi, x, core).
Axes of the slice: x: 4, y: 4, z: 16 (z_hi: 4, z_lo: 4; z = z_hi * 4 + z_lo), core: 2. Of those that a mesh axis runs over, the one named last changes fastest.
Arguments:
- vof: bfloat16 [6144, 512], P(('stream', 'cross')), may hold values from 0 to 1
- target: bfloat16 [6144, 512], P(('stream', 'cross')), may hold values from -21 to 21
- neighbours: int32 [6144, 26], P(('stream', 'cross')), may hold values from -1 to 6143, as said below
- live_blocks: int32 [512], P(('stream', 'cross')), may hold values from 2 to 12, as said below
- pick: int32 [512, 2], P(('stream', 'cross')), may hold values from -1 to 191, as said below
- w_first: bfloat16 [125, 128], replicated, may hold values from -0.5 to 0.5
- w_mid: bfloat16 [2, 128, 128], replicated, may hold values from -0.5 to 0.5
- w_last: bfloat16 [128], replicated, may hold values from -0.5 to 0.5
Outputs:
- prediction: float32 [4096, 512], P(('stream', 'cross'))
- grad_first: float32 [125, 128], replicated
- grad_mid: float32 [2, 128, 128], replicated
- grad_last: float32 [128], replicated
Inputs may be any that keep to these rules, and one draw needn't show every extreme that they name: Home slots 0 to live_blocks[d] - 1 of device d hold interface blocks and the rest are empty; in every slab 8 devices hold more than 6 blocks and the others at most 6. `neighbours`: an entry names a live home slot of a device whose stream index and cross index each differ from those of the block's own device by at most one. `pick`: in each slab every live home slot 6 + j of the device with cross index c is named, as c * 6 + j, by exactly one entry of one device of that slab; devices holding more than 6 blocks name none.
All inputs are finite; a program needn't handle non-finite values.
Results may differ from a plain program's by a relative error of at most 0.003.
The roundings to bfloat16 on the way count: a program that leaves them out, or rounds other values in their place, can miss the bound.
Values may be sent and summed in bfloat16 or wider, within the bound.
A program may use at most 128 MiB of HBM per device.

v0:
```python
import jax
import jax.numpy as jnp
from jax import lax
from jax.sharding import PartitionSpec as P

FEAT = 125
BE = 8
KEEP = 6
RECV = 2
PADROW = 1792


def from_behind(block, axis, distance):
    devices = range(lax.axis_size(axis))
    route = [(i - distance, i) for i in devices if i - distance in devices]
    return lax.ppermute(block, axis, route)


def assemble(center, border, block_edge):
    number = center.shape[0]
    pieces = jnp.concatenate([border[:, :13], center[:, None], border[:, 13:]], axis=1)
    shaped = pieces.reshape(number, 3, 3, 3, block_edge, block_edge, block_edge)
    shaped = shaped.transpose(0, 1, 4, 2, 5, 3, 6).reshape(
        number, 3 * block_edge, 3 * block_edge, 3 * block_edge
    )
    lower = block_edge - 2
    upper = 2 * block_edge + 2
    return shaped[:, lower:upper, lower:upper, lower:upper]


def stencil(padded, block_edge):
    columns = []
    for along_x in range(5):
        for along_y in range(5):
            for along_z in range(5):
                window = padded[
                    :,
                    along_x : along_x + block_edge,
                    along_y : along_y + block_edge,
                    along_z : along_z + block_edge,
                ]
                columns.append(window.reshape(-1))
    return jnp.stack(columns)


def contract_rows(former, latter):
    return lax.dot_general(
        former, latter, (((0,), (0,)), ((), ())), preferred_element_type=jnp.float32
    )


def contract_cols(former, latter):
    return lax.dot_general(
        former, latter, (((1,), (1,)), ((), ())), preferred_element_type=jnp.float32
    )


def train_terms(features, target_row, weight_mask, w_first, w_mid, w_last, loss_scale):
    hidden_one = jnp.tanh(contract_rows(w_first, features)).astype(jnp.bfloat16)
    hidden_two = jnp.tanh(contract_rows(w_mid[0], hidden_one)).astype(jnp.bfloat16)
    hidden_three = jnp.tanh(contract_rows(w_mid[1], hidden_two)).astype(jnp.bfloat16)
    predicted = jnp.dot(w_last, hidden_three, preferred_element_type=jnp.float32) * weight_mask
    residual = ((predicted - target_row.astype(jnp.float32)) * weight_mask / loss_scale).astype(
        jnp.bfloat16
    )
    grad_last = jnp.dot(hidden_three, residual, preferred_element_type=jnp.float32)
    slope_three = 1.0 - jnp.square(hidden_three.astype(jnp.float32))
    delta_three = (
        w_last.astype(jnp.float32)[:, None] * residual.astype(jnp.float32)[None, :] * slope_three
    ).astype(jnp.bfloat16)
    grad_third = contract_cols(hidden_two, delta_three)
    slope_two = 1.0 - jnp.square(hidden_two.astype(jnp.float32))
    delta_two = (
        jnp.dot(w_mid[1], delta_three, preferred_element_type=jnp.float32) * slope_two
    ).astype(jnp.bfloat16)
    grad_second = contract_cols(hidden_one, delta_two)
    slope_one = 1.0 - jnp.square(hidden_one.astype(jnp.float32))
    delta_one = (
        jnp.dot(w_mid[0], delta_two, preferred_element_type=jnp.float32) * slope_one
    ).astype(jnp.bfloat16)
    grad_first = contract_cols(features, delta_one)
    return (predicted, grad_first, jnp.stack([grad_second, grad_third]), grad_last)


def shards(vof, target, neighbours, live_blocks, pick, w_first, w_mid, w_last):
    home_blocks = vof.shape[0]
    cell_count = vof.shape[1]
    cross_size = lax.axis_size("cross")
    stream_size = lax.axis_size("stream")
    slab_index = lax.axis_index("stream")
    cross_index = lax.axis_index("cross")
    below = from_behind(vof, "stream", 1)
    above = from_behind(vof, "stream", -1)
    column = jnp.stack([below, vof, above])
    left = from_behind(column, "cross", 1)
    right = from_behind(column, "cross", -1)
    beside_all = jnp.stack([left, column, right], axis=1)
    table = jnp.concatenate(
        [beside_all.reshape(9 * home_blocks, cell_count), jnp.zeros((1, cell_count), vof.dtype)],
        axis=0,
    )
    owner_device = neighbours // home_blocks
    slab_step = owner_device // cross_size - slab_index + 1
    cross_step = owner_device % cross_size - cross_index + 1
    lookup = (slab_step * 3 + cross_step) * home_blocks + neighbours % home_blocks
    lookup = jnp.where(neighbours < 0, 9 * home_blocks, lookup)
    border = jnp.take(table, lookup, axis=0)
    padded = assemble(vof, border, BE)
    live_count = live_blocks[0]
    home_mask = (jnp.arange(home_blocks) < live_count).astype(jnp.float32)
    loss_scale = float(cell_count * KEEP * cross_size * stream_size)
    chosen = pick[0]
    padded_edge = padded.shape[1]
    flat_rows = padded.reshape(home_blocks, padded_edge**3)
    flat_rows = jnp.pad(flat_rows, ((0, 0), (0, PADROW - padded_edge**3)))
    pieces = (
        lax.all_gather(flat_rows[KEEP:], "cross", axis=0, tiled=True),
        lax.all_gather(target[KEEP:], "cross", axis=0, tiled=True),
    )
    selector = (chosen[:, None] == jnp.arange(pieces[0].shape[0])[None, :]).astype(jnp.bfloat16)
    got_blocks = jnp.dot(selector, pieces[0], preferred_element_type=jnp.float32)
    got_targets = jnp.dot(selector, pieces[1], preferred_element_type=jnp.float32)
    got_blocks = got_blocks.astype(jnp.bfloat16)
    got_targets = got_targets.astype(jnp.bfloat16)
    got_blocks = got_blocks[:, : padded_edge**3].reshape(
        RECV, padded_edge, padded_edge, padded_edge
    )
    work_padded = jnp.concatenate([padded[:KEEP], got_blocks], axis=0)
    work_target = jnp.concatenate([target[:KEEP], got_targets], axis=0)
    block_mask = jnp.concatenate([home_mask[:KEEP], (chosen >= 0).astype(jnp.float32)])
    predicted, grad_first, grad_mid, grad_last = train_terms(
        stencil(work_padded, BE),
        work_target.reshape(-1),
        jnp.repeat(block_mask, cell_count),
        w_first,
        w_mid,
        w_last,
        loss_scale,
    )
    prediction = predicted.reshape(KEEP + RECV, cell_count)
    hidden_size = grad_last.shape[0]
    packed = jnp.concatenate(
        [
            grad_first,
            grad_last[None, :],
            jnp.zeros((128 - FEAT - 1, hidden_size), jnp.float32),
            grad_mid.reshape(2 * hidden_size, hidden_size),
        ],
        axis=0,
    )
    summed = lax.psum(packed, ("stream", "cross"))
    return (
        prediction,
        summed[:FEAT],
        summed[128:].reshape(2, hidden_size, hidden_size),
        summed[FEAT],
    )


def solution(mesh):
    return jax.shard_map(
        shards,
        mesh=mesh,
        in_specs=(
            P(("stream", "cross"), None),
            P(("stream", "cross"), None),
            P(("stream", "cross"), None),
            P(("stream", "cross")),
            P(("stream", "cross"), None),
            P(),
            P(),
            P(),
        ),
        out_specs=(P(("stream", "cross"), None), P(), P(), P()),
        check_vma=False,
    )
```

profile of v0, /device:TPU:1, one launch (start us, length us, event | category | flops | bytes accessed | tf_op | source)
XLA Modules:
  0.0 796.8 jit_solution(742776914680141394)
XLA Ops:
  7.2 4.0 collective-permute-start
  11.3 1.3 collective-permute-start.1
  13.4 60.5 %all-gather.1 = bf16[32,6,512]{2,1,0:T(8,128)(2,1)S(1)} all-gather(bf16[1,6,512]{2,1,0:T(8,128)(2,1)S(1)} %get-tuple-element.139), channel_id=1, replica_groups=mesh['stream'=16,'cross'=32] {'cross'}, dimensions={0}, use_global_device_ids=true | all-gather | bytes 202752 | tf_op jit(solution)/shard_map/all_gather | solution.py:118
  77.8 1.9 collective-permute-start.2
  79.7 2.4 collective-permute-start.3
  84.1 1.2 convert_element_type.65
  86.1 2.0 gather_fusion
  88.6 7.5 reshape.47
  96.0 12.7 %copy.151 = bf16[12,3,8,3,8,3,8]{0,6,5,4,3,2,1:T(8,128)(2,1)} copy(bf16[12,3,8,3,8,3,8]{6,4,2,5,3,1,0:T(8,128)(2,1)} %bitcast.318) | data formatting | bytes 663552 | tf_op jit(solution)/shard_map/transpose | solution.py:23
  108.7 1.4 slice.565
  110.2 1.4 slice.564
  112.1 53.0 %all-gather = bf16[32,6,1792]{2,1,0:T(8,128)(2,1)S(1)} all-gather(bf16[1,6,1792]{2,1,0:T(8,128)(2,1)S(1)} %fusion.18), channel_id=1, replica_groups=mesh['stream'=16,'cross'=32] {'cross'}, dimensions={0}, use_global_device_ids=true | all-gather | bytes 709632 | tf_op jit(solution)/shard_map/all_gather | solution.py:117
  167.3 1.2 slice_maximum_fusion.12
  168.4 1.2 slice_maximum_fusion.13
  169.6 1.2 slice_maximum_fusion.14
  170.8 1.3 slice_maximum_fusion.15
  172.1 1.2 slice_maximum_fusion.16
  174.5 1.2 slice_maximum_fusion.18
  175.7 1.3 slice_maximum_fusion.19
  176.9 1.3 slice_maximum_fusion.20
  178.2 1.3 slice_maximum_fusion.21
  179.4 1.3 slice_maximum_fusion.22
  180.7 1.1 slice_maximum_fusion.23
  181.8 1.3 slice_maximum_fusion.24
  183.1 1.3 slice_maximum_fusion.25
  184.4 1.3 slice_maximum_fusion.26
  185.6 1.3 slice_maximum_fusion.27
  186.9 1.2 slice_maximum_fusion.28
  188.0 1.2 slice_maximum_fusion.29
  189.2 1.2 slice_maximum_fusion.11
  190.4 1.3 slice_maximum_fusion.10
  191.6 1.2 slice_maximum_fusion.9
  192.9 1.1 slice_maximum_fusion.8
  194.0 1.4 slice_maximum_fusion.7
  195.4 1.2 slice_maximum_fusion.6
  196.6 1.3 slice_maximum_fusion.5
  197.9 1.2 slice_maximum_fusion.4
  199.1 1.1 slice_maximum_fusion.3
  209.2 1.2 copy.200
  281.1 1.2 copy.191
  310.7 9.6 %stack.44 = bf16[125,4096]{1,0:T(8,128)(2,1)S(1)} concatenate(bf16[1,4096]{1,0:T(2,128)(2,1)S(1)} %stack_reshape.375, bf16[1,4096]{1,0:T(2,128)(2,1)S(1)} %stack_reshape.376, bf16[1,4096]{1,0:T(2,128)(2,1)S(1)} %stack_reshape.377, bf16[1,4096]{1,0:T(2,128)(2,1)S(1)} %stack_reshape.378, bf16[1,4096]{1,0:T(2,128)(2,1)S(1)} %stack_reshape.379, bf16[1,4096]{1,0:T(2,128)(2,1)S(1)} %stack_reshape.380, ...), dimensions={0} | concatenate | bytes 2048000 | tf_op jit(solution)/shard_map/stack | solution.py:43
  322.2 1.8 fusion.3
  324.0 2.1 fusion.6
  326.1 1.8 convolution_bitcast_fusion.1
  330.7 454.9 %all-reduce.4.cloned.1.call-done = f32[384,128]{1,0:T(8,128)} async-done(((f32[384,128]{1,0:T(8,128)}), f32[384,128]{1,0:T(8,128)}) %all-reduce.4.cloned.1.call-update) | async-done | bytes 196624 | tf_op jit(solution)/shard_map/psum | solution.py:151
  785.5 1.6 slice.816
  787.1 1.5 slice.815
  788.6 1.2 slice_bitcast_fusion.1
  (610 shorter events, 121.2 us)
Async XLA Ops:
  7.2 313.1 %copy-start = (bf16[125,128]{1,0:T(8,128)(2,1)S(1)}, bf16[125,128]{1,0:T(8,128)(2,1)}, u32[]{:S(2)}) copy-start(bf16[125,128]{1,0:T(8,128)(2,1)} %param.13) | copy-start | bytes 96004
  7.2 778.4 %all-reduce.4.cloned.1.call-start = ((), (), s32[]{:S(2)}) async-start(), calls=%async_computation | async-start | bytes 393216 | tf_op jit(solution)/shard_map/psum | solution.py:151
  7.2 69.8 %collective-permute-start = (bf16[12,512]{1,0:T(8,128)(2,1)}, bf16[12,512]{1,0:T(8,128)(2,1)S(1)}, u32[]{:S(2)}, u32[]{:S(2)}) collective-permute-start(bf16[12,512]{1,0:T(8,128)(2,1)} %param.8), channel_id=1, source_target_pairs={{0,32},{32,64},{64,96},{96,128},{128,160},{160,192},{192,224},{224... | collective-permute-start | bytes 36872 | tf_op jit(solution)/shard_map/ppermute | solution.py:16
  11.3 65.8 %collective-permute-start.1 = (bf16[12,512]{1,0:T(8,128)(2,1)}, bf16[12,512]{1,0:T(8,128)(2,1)S(1)}, u32[]{:S(2)}, u32[]{:S(2)}) collective-permute-start(bf16[12,512]{1,0:T(8,128)(2,1)} %param.8), channel_id=1, source_target_pairs={{32,0},{64,32},{96,64},{128,96},{160,128},{192,160},{224,192},{256... | collective-permute-start | bytes 36872 | tf_op jit(solution)/shard_map/ppermute | solution.py:16
  77.8 8.2 %collective-permute-start.2 = (bf16[3,12,512]{2,1,0:T(8,128)(2,1)S(1)}, bf16[3,12,512]{2,1,0:T(8,128)(2,1)S(1)}, u32[]{:S(2)}, u32[]{:S(2)}) collective-permute-start(bf16[3,12,512]{2,1,0:T(8,128)(2,1)S(1)} %get-tuple-element.137), channel_id=1, source_target_pairs={{0,1},{1,2},{2,3},{3,4},{4,5},{5,6},{6,7},{7,8},{8,9},{9,10},{10,1... | collective-permute-start | bytes 110600 | tf_op jit(solution)/shard_map/ppermute | solution.py:16
  79.7 6.2 collective-permute-start.3
  111.6 53.7 %copy-start.151 = (s32[1,2]{1,0:T(1,128)S(1)}, s32[1,2]{1,0:T(1,128)}, u32[]{:S(2)}) copy-start(s32[1,2]{1,0:T(1,128)} %param.12) | copy-start | bytes 28
  204.8 11.7 %copy-start.97 = (bf16[8,8,8,8]{0,3,2,1:T(8,128)(2,1)S(1)}, bf16[8,8,8,8]{0,3,2,1:T(8,128)(2,1)}, u32[]{:S(2)}) copy-start(bf16[8,8,8,8]{0,3,2,1:T(8,128)(2,1)} %get-tuple-element.79) | copy-start | bytes 24580
  205.2 12.3 %copy-start.96 = (bf16[8,8,8,8]{0,3,2,1:T(8,128)(2,1)S(1)}, bf16[8,8,8,8]{0,3,2,1:T(8,128)(2,1)}, u32[]{:S(2)}) copy-start(bf16[8,8,8,8]{0,3,2,1:T(8,128)(2,1)} %get-tuple-element.80) | copy-start | bytes 24580
  206.3 12.3 %copy-start.95 = (bf16[8,8,8,8]{0,3,2,1:T(8,128)(2,1)S(1)}, bf16[8,8,8,8]{0,3,2,1:T(8,128)(2,1)}, u32[]{:S(2)}) copy-start(bf16[8,8,8,8]{0,3,2,1:T(8,128)(2,1)} %get-tuple-element.81) | copy-start | bytes 24580
  207.4 12.3 %copy-start.94 = (bf16[8,8,8,8]{0,3,2,1:T(8,128)(2,1)S(1)}, bf16[8,8,8,8]{0,3,2,1:T(8,128)(2,1)}, u32[]{:S(2)}) copy-start(bf16[8,8,8,8]{0,3,2,1:T(8,128)(2,1)} %get-tuple-element.83) | copy-start | bytes 24580
  208.4 12.3 %copy-start.93 = (bf16[8,8,8,8]{0,3,2,1:T(8,128)(2,1)S(1)}, bf16[8,8,8,8]{0,3,2,1:T(8,128)(2,1)}, u32[]{:S(2)}) copy-start(bf16[8,8,8,8]{0,3,2,1:T(8,128)(2,1)} %get-tuple-element.84) | copy-start | bytes 24580
  210.4 11.5 %copy-start.92 = (bf16[8,8,8,8]{0,3,2,1:T(8,128)(2,1)S(1)}, bf16[8,8,8,8]{0,3,2,1:T(8,128)(2,1)}, u32[]{:S(2)}) copy-start(bf16[8,8,8,8]{0,3,2,1:T(8,128)(2,1)} %get-tuple-element.85) | copy-start | bytes 24580
  211.5 11.5 %copy-start.91 = (bf16[8,8,8,8]{0,3,2,1:T(8,128)(2,1)S(1)}, bf16[8,8,8,8]{0,3,2,1:T(8,128)(2,1)}, u32[]{:S(2)}) copy-start(bf16[8,8,8,8]{0,3,2,1:T(8,128)(2,1)} %get-tuple-element.87) | copy-start | bytes 24580
  212.5 11.5 %copy-start.90 = (bf16[8,8,8,8]{0,3,2,1:T(8,128)(2,1)S(1)}, bf16[8,8,8,8]{0,3,2,1:T(8,128)(2,1)}, u32[]{:S(2)}) copy-start(bf16[8,8,8,8]{0,3,2,1:T(8,128)(2,1)} %get-tuple-element.88) | copy-start | bytes 24580
  213.6 11.7 %copy-start.89 = (bf16[8,8,8,8]{0,3,2,1:T(8,128)(2,1)S(1)}, bf16[8,8,8,8]{0,3,2,1:T(8,128)(2,1)}, u32[]{:S(2)}) copy-start(bf16[8,8,8,8]{0,3,2,1:T(8,128)(2,1)} %get-tuple-element.89) | copy-start | bytes 24580
  214.7 11.7 %copy-start.88 = (bf16[8,8,8,8]{0,3,2,1:T(8,128)(2,1)S(1)}, bf16[8,8,8,8]{0,3,2,1:T(8,128)(2,1)}, u32[]{:S(2)}) copy-start(bf16[8,8,8,8]{0,3,2,1:T(8,128)(2,1)} %get-tuple-element.91) | copy-start | bytes 24580
  215.7 11.7 %copy-start.87 = (bf16[8,8,8,8]{0,3,2,1:T(8,128)(2,1)S(1)}, bf16[8,8,8,8]{0,3,2,1:T(8,128)(2,1)}, u32[]{:S(2)}) copy-start(bf16[8,8,8,8]{0,3,2,1:T(8,128)(2,1)} %get-tuple-element.92) | copy-start | bytes 24580
  216.8 11.7 %copy-start.86 = (bf16[8,8,8,8]{0,3,2,1:T(8,128)(2,1)S(1)}, bf16[8,8,8,8]{0,3,2,1:T(8,128)(2,1)}, u32[]{:S(2)}) copy-start(bf16[8,8,8,8]{0,3,2,1:T(8,128)(2,1)} %get-tuple-element.93) | copy-start | bytes 24580
  217.9 11.7 %copy-start.85 = (bf16[8,8,8,8]{0,3,2,1:T(8,128)(2,1)S(1)}, bf16[8,8,8,8]{0,3,2,1:T(8,128)(2,1)}, u32[]{:S(2)}) copy-start(bf16[8,8,8,8]{0,3,2,1:T(8,128)(2,1)} %get-tuple-element.95) | copy-start | bytes 24580
  218.9 11.6 %copy-start.84 = (bf16[8,8,8,8]{0,3,2,1:T(8,128)(2,1)S(1)}, bf16[8,8,8,8]{0,3,2,1:T(8,128)(2,1)}, u32[]{:S(2)}) copy-start(bf16[8,8,8,8]{0,3,2,1:T(8,128)(2,1)} %get-tuple-element.96) | copy-start | bytes 24580
  220.0 11.6 %copy-start.83 = (bf16[8,8,8,8]{0,3,2,1:T(8,128)(2,1)S(1)}, bf16[8,8,8,8]{0,3,2,1:T(8,128)(2,1)}, u32[]{:S(2)}) copy-start(bf16[8,8,8,8]{0,3,2,1:T(8,128)(2,1)} %get-tuple-element.97) | copy-start | bytes 24580
  221.1 11.6 %copy-start.82 = (bf16[8,8,8,8]{0,3,2,1:T(8,128)(2,1)S(1)}, bf16[8,8,8,8]{0,3,2,1:T(8,128)(2,1)}, u32[]{:S(2)}) copy-start(bf16[8,8,8,8]{0,3,2,1:T(8,128)(2,1)} %get-tuple-element.99) | copy-start | bytes 24580
  222.1 11.7 %copy-start.81 = (bf16[8,8,8,8]{0,3,2,1:T(8,128)(2,1)S(1)}, bf16[8,8,8,8]{0,3,2,1:T(8,128)(2,1)}, u32[]{:S(2)}) copy-start(bf16[8,8,8,8]{0,3,2,1:T(8,128)(2,1)} %get-tuple-element.100) | copy-start | bytes 24580
  223.2 11.6 %copy-start.80 = (bf16[8,8,8,8]{0,3,2,1:T(8,128)(2,1)S(1)}, bf16[8,8,8,8]{0,3,2,1:T(8,128)(2,1)}, u32[]{:S(2)}) copy-start(bf16[8,8,8,8]{0,3,2,1:T(8,128)(2,1)} %get-tuple-element.101) | copy-start | bytes 24580
  228.8 11.5 %copy-start.75 = (bf16[8,8,8,8]{0,3,2,1:T(8,128)(2,1)S(1)}, bf16[8,8,8,8]{0,3,2,1:T(8,128)(2,1)}, u32[]{:S(2)}) copy-start(bf16[8,8,8,8]{0,3,2,1:T(8,128)(2,1)} %get-tuple-element.108) | copy-start | bytes 24580
  230.9 11.5 %copy-start.73 = (bf16[8,8,8,8]{0,3,2,1:T(8,128)(2,1)S(1)}, bf16[8,8,8,8]{0,3,2,1:T(8,128)(2,1)}, u32[]{:S(2)}) copy-start(bf16[8,8,8,8]{0,3,2,1:T(8,128)(2,1)} %get-tuple-element.111) | copy-start | bytes 24580
  244.8 11.5 %copy-start.60 = (bf16[8,8,8,8]{0,3,2,1:T(8,128)(2,1)S(1)}, bf16[8,8,8,8]{0,3,2,1:T(8,128)(2,1)}, u32[]{:S(2)}) copy-start(bf16[8,8,8,8]{0,3,2,1:T(8,128)(2,1)} %get-tuple-element.128) | copy-start | bytes 24580
  245.8 11.5 %copy-start.59 = (bf16[8,8,8,8]{0,3,2,1:T(8,128)(2,1)S(1)}, bf16[8,8,8,8]{0,3,2,1:T(8,128)(2,1)}, u32[]{:S(2)}) copy-start(bf16[8,8,8,8]{0,3,2,1:T(8,128)(2,1)} %get-tuple-element.129) | copy-start | bytes 24580
  246.9 11.5 %copy-start.58 = (bf16[8,8,8,8]{0,3,2,1:T(8,128)(2,1)S(1)}, bf16[8,8,8,8]{0,3,2,1:T(8,128)(2,1)}, u32[]{:S(2)}) copy-start(bf16[8,8,8,8]{0,3,2,1:T(8,128)(2,1)} %get-tuple-element.131) | copy-start | bytes 24580
  248.0 11.5 %copy-start.57 = (bf16[8,8,8,8]{0,3,2,1:T(8,128)(2,1)S(1)}, bf16[8,8,8,8]{0,3,2,1:T(8,128)(2,1)}, u32[]{:S(2)}) copy-start(bf16[8,8,8,8]{0,3,2,1:T(8,128)(2,1)} %get-tuple-element.132) | copy-start | bytes 24580
  250.1 11.8 %copy-start.55 = (bf16[8,8,8,8]{0,3,2,1:T(8,128)(2,1)S(1)}, bf16[8,8,8,8]{0,3,2,1:T(8,128)(2,1)}, u32[]{:S(2)}) copy-start(bf16[8,8,8,8]{0,3,2,1:T(8,128)(2,1)} %get-tuple-element.130) | copy-start | bytes 24580
  251.2 11.8 %copy-start.54 = (bf16[8,8,8,8]{0,3,2,1:T(8,128)(2,1)S(1)}, bf16[8,8,8,8]{0,3,2,1:T(8,128)(2,1)}, u32[]{:S(2)}) copy-start(bf16[8,8,8,8]{0,3,2,1:T(8,128)(2,1)} %get-tuple-element.126) | copy-start | bytes 24580
  252.2 11.8 %copy-start.53 = (bf16[8,8,8,8]{0,3,2,1:T(8,128)(2,1)S(1)}, bf16[8,8,8,8]{0,3,2,1:T(8,128)(2,1)}, u32[]{:S(2)}) copy-start(bf16[8,8,8,8]{0,3,2,1:T(8,128)(2,1)} %get-tuple-element.122) | copy-start | bytes 24580
  253.3 11.8 %copy-start.52 = (bf16[8,8,8,8]{0,3,2,1:T(8,128)(2,1)S(1)}, bf16[8,8,8,8]{0,3,2,1:T(8,128)(2,1)}, u32[]{:S(2)}) copy-start(bf16[8,8,8,8]{0,3,2,1:T(8,128)(2,1)} %get-tuple-element.118) | copy-start | bytes 24580
  254.4 11.8 %copy-start.51 = (bf16[8,8,8,8]{0,3,2,1:T(8,128)(2,1)S(1)}, bf16[8,8,8,8]{0,3,2,1:T(8,128)(2,1)}, u32[]{:S(2)}) copy-start(bf16[8,8,8,8]{0,3,2,1:T(8,128)(2,1)} %get-tuple-element.114) | copy-start | bytes 24580
  255.4 11.8 %copy-start.50 = (bf16[8,8,8,8]{0,3,2,1:T(8,128)(2,1)S(1)}, bf16[8,8,8,8]{0,3,2,1:T(8,128)(2,1)}, u32[]{:S(2)}) copy-start(bf16[8,8,8,8]{0,3,2,1:T(8,128)(2,1)} %get-tuple-element.110) | copy-start | bytes 24580
  256.5 11.8 %copy-start.49 = (bf16[8,8,8,8]{0,3,2,1:T(8,128)(2,1)S(1)}, bf16[8,8,8,8]{0,3,2,1:T(8,128)(2,1)}, u32[]{:S(2)}) copy-start(bf16[8,8,8,8]{0,3,2,1:T(8,128)(2,1)} %get-tuple-element.106) | copy-start | bytes 24580
  257.6 11.8 %copy-start.48 = (bf16[8,8,8,8]{0,3,2,1:T(8,128)(2,1)S(1)}, bf16[8,8,8,8]{0,3,2,1:T(8,128)(2,1)}, u32[]{:S(2)}) copy-start(bf16[8,8,8,8]{0,3,2,1:T(8,128)(2,1)} %get-tuple-element.102) | copy-start | bytes 24580
  258.6 11.8 %copy-start.47 = (bf16[8,8,8,8]{0,3,2,1:T(8,128)(2,1)S(1)}, bf16[8,8,8,8]{0,3,2,1:T(8,128)(2,1)}, u32[]{:S(2)}) copy-start(bf16[8,8,8,8]{0,3,2,1:T(8,128)(2,1)} %get-tuple-element.98) | copy-start | bytes 24580
  259.7 11.8 %copy-start.46 = (bf16[8,8,8,8]{0,3,2,1:T(8,128)(2,1)S(1)}, bf16[8,8,8,8]{0,3,2,1:T(8,128)(2,1)}, u32[]{:S(2)}) copy-start(bf16[8,8,8,8]{0,3,2,1:T(8,128)(2,1)} %get-tuple-element.94) | copy-start | bytes 24580
  262.2 11.5 %copy-start.37 = (bf16[8,8,8,8]{0,3,2,1:T(8,128)(2,1)S(1)}, bf16[8,8,8,8]{0,3,2,1:T(8,128)(2,1)}, u32[]{:S(2)}) copy-start(bf16[8,8,8,8]{0,3,2,1:T(8,128)(2,1)} %get-tuple-element.86) | copy-start | bytes 24580
  264.3 11.5 %copy-start.28 = (bf16[8,8,8,8]{0,3,2,1:T(8,128)(2,1)S(1)}, bf16[8,8,8,8]{0,3,2,1:T(8,128)(2,1)}, u32[]{:S(2)}) copy-start(bf16[8,8,8,8]{0,3,2,1:T(8,128)(2,1)} %get-tuple-element.78) | copy-start | bytes 24580
  266.5 11.5 %copy-start.20 = (bf16[8,8,8,8]{0,3,2,1:T(8,128)(2,1)S(1)}, bf16[8,8,8,8]{0,3,2,1:T(8,128)(2,1)}, u32[]{:S(2)}) copy-start(bf16[8,8,8,8]{0,3,2,1:T(8,128)(2,1)} %get-tuple-element.70) | copy-start | bytes 24580
  267.6 11.5 %copy-start.15 = (bf16[8,8,8,8]{0,3,2,1:T(8,128)(2,1)S(1)}, bf16[8,8,8,8]{0,3,2,1:T(8,128)(2,1)}, u32[]{:S(2)}) copy-start(bf16[8,8,8,8]{0,3,2,1:T(8,128)(2,1)} %get-tuple-element.66) | copy-start | bytes 24580
  268.6 11.5 %copy-start.11 = (bf16[8,8,8,8]{0,3,2,1:T(8,128)(2,1)S(1)}, bf16[8,8,8,8]{0,3,2,1:T(8,128)(2,1)}, u32[]{:S(2)}) copy-start(bf16[8,8,8,8]{0,3,2,1:T(8,128)(2,1)} %get-tuple-element.62) | copy-start | bytes 24580
  270.8 12.4 %copy-start.45 = (bf16[8,8,8,8]{0,3,2,1:T(8,128)(2,1)S(1)}, bf16[8,8,8,8]{0,3,2,1:T(8,128)(2,1)}, u32[]{:S(2)}) copy-start(bf16[8,8,8,8]{0,3,2,1:T(8,128)(2,1)} %get-tuple-element.60) | copy-start | bytes 24580
  271.8 11.8 %copy-start.44 = (bf16[8,8,8,8]{0,3,2,1:T(8,128)(2,1)S(1)}, bf16[8,8,8,8]{0,3,2,1:T(8,128)(2,1)}, u32[]{:S(2)}) copy-start(bf16[8,8,8,8]{0,3,2,1:T(8,128)(2,1)} %get-tuple-element.61) | copy-start | bytes 24580
  (111 other events, 775.7 us)
Sparse Core Ops, SparseCore 0:
  330.2 455.2 all-reduce.3
where the time goes:
time: 803 us; the launch traced here: 797 us
  waiting for transfers between devices  455 us (57%)
  local copies, waits for them, and re-layouts  152 us (19%)
  blocking collectives  114 us (14%)
  other arithmetic  39.4 us (5%)
  between operations  17.8 us (2%)
  matrix products  9.76 us (1%)
  starting transfers between devices  9.69 us (1%)
    psum x1, waiting for transfers between devices, shards(): summed = lax.psum(packed, ('stream', 'cross'))  455 us
    another operation x126, local copies, waits for them, and re-layouts, stencil(): return jnp.stack(columns)  77.5 us
    all_gather x1, blocking collectives, shards(): lax.all_gather(target[KEEP:], 'cross', axis=0, tiled=True)  60.5 us
    all_gather x1, blocking collectives, shards(): lax.all_gather(flat_rows[KEEP:], 'cross', axis=0, tiled=True)  53 us
    slice x125, local copies, waits for them, and re-layouts, stencil(): padded[:, along_x:along_x + block_edge, along_y:along_y + block_edge, alo...  38.1 us
    concatenate x31, other arithmetic, shards(): work_padded = jnp.concatenate([padded[:KEEP], got_blocks], axis=0)  34.8 us
  transfers between devices with their start and end apart: 5, of which 1 were waited for; matrix products, arithmetic and copies ran while one was open for 1% of the time, Pallas kernels for 0%

commit v1 on v0

--- a/solution.py
+++ b/solution.py
@@ -148,7 +148,7 @@
         ],
         axis=0,
     )
-    summed = lax.psum(packed, ("stream", "cross"))
+    summed = jnp.sum(lax.all_gather(packed, ("stream", "cross")), axis=0)
     return (
         prediction,
         summed[:FEAT],

time: 803 us -> 1360 us (1.69)
  waiting for transfers between devices: 455 us -> 940 us
  local copies, waits for them, and re-layouts: 152 us -> 194 us
  other arithmetic: 39.4 us -> 70.2 us
    all_gather x0 -> x1, waiting for transfers between devices: none -> 940 us  [shards(): summed = jnp.sum(lax.all_gather(packed, ('stream', 'cross')), axis=0)]
    psum x1 -> x0, waiting for transfers between devices: 455 us -> none  [shards(): summed = lax.psum(packed, ('stream', 'cross'))]
    reduce_sum x0 -> x1, other arithmetic: none -> 30.9 us  [shards(): summed = jnp.sum(lax.all_gather(packed, ('stream', 'cross')), axis=0)]
    slice x125, local copies, waits for them, and re-layouts: 38.1 us -> 65.4 us  [stencil(): padded[:, along_x:along_x + block_edge, along_y:along_y + block_edge, alo...]
    another operation x126, local copies, waits for them, and re-layouts: 77.5 us -> 94.4 us  [stencil(): return jnp.stack(columns)]
where the time goes in v1:
time: 1360 us; the launch traced here: 1350 us
  waiting for transfers between devices  940 us (69%)
  local copies, waits for them, and re-layouts  194 us (14%)
  blocking collectives  111 us (8%)
  other arithmetic  70.2 us (5%)
  between operations  17.8 us (1%)
    all_gather x1, waiting for transfers between devices, shards(): summed = jnp.sum(lax.all_gather(packed, ('stream', 'cross')), axis=0)  940 us
    another operation x126, local copies, waits for them, and re-layouts, stencil(): return jnp.stack(columns)  94.4 us
    slice x125, local copies, waits for them, and re-layouts, stencil(): padded[:, along_x:along_x + block_edge, along_y:along_y + block_edge, alo...  65.4 us
    all_gather x1, blocking collectives, shards(): lax.all_gather(target[KEEP:], 'cross', axis=0, tiled=True)  60.5 us
    all_gather x1, blocking collectives, shards(): lax.all_gather(flat_rows[KEEP:], 'cross', axis=0, tiled=True)  50.4 us
    concatenate x31, other arithmetic, shards(): work_padded = jnp.concatenate([padded[:KEEP], got_blocks], axis=0)  34.7 us
    reduce_sum x1, other arithmetic, shards(): summed = jnp.sum(lax.all_gather(packed, ('stream', 'cross')), axis=0)  30.9 us
  transfers between devices with their start and end apart: 5, of which 1 were waited for; matrix products, arithmetic and copies ran while one was open for 1% of the time, Pallas kernels for 0%

profile of v1, /device:TPU:1, one launch (start us, length us, event | category | flops | bytes accessed | tf_op | source)
XLA Modules:
  0.0 1353.1 jit_solution(5195124274105249857)
XLA Ops:
  7.2 4.0 collective-permute-start
  11.3 1.3 collective-permute-start.1
  14.8 60.5 %all-gather.2 = bf16[32,6,512]{2,1,0:T(8,128)(2,1)S(1)} all-gather(bf16[1,6,512]{2,1,0:T(8,128)(2,1)S(1)} %get-tuple-element.139), channel_id=1, replica_groups=mesh['stream'=16,'cross'=32] {'cross'}, dimensions={0}, use_global_device_ids=true | all-gather | bytes 202752 | tf_op jit(solution)/shard_map/all_gather | solution.py:118
  77.8 2.1 collective-permute-start.3
  79.9 3.5 collective-permute-start.2
  87.3 2.0 gather_fusion
  89.8 7.4 reshape.47
  97.2 12.7 copy.151
  110.0 1.4 slice.564
  111.4 1.4 slice.565
  113.3 50.4 %all-gather.1 = bf16[32,6,1792]{2,1,0:T(8,128)(2,1)S(1)} all-gather(bf16[1,6,1792]{2,1,0:T(8,128)(2,1)S(1)} %fusion.18), channel_id=1, replica_groups=mesh['stream'=16,'cross'=32] {'cross'}, dimensions={0}, use_global_device_ids=true | all-gather | bytes 709632 | tf_op jit(solution)/shard_map/all_gather | solution.py:117
  167.6 1.2 slice_maximum_fusion.27
  168.8 1.2 slice_maximum_fusion.26
  170.1 1.3 slice_maximum_fusion.25
  171.4 1.2 slice_maximum_fusion.24
  172.6 1.2 slice_maximum_fusion.23
  173.8 1.2 slice_maximum_fusion.22
  175.0 1.2 slice_maximum_fusion.21
  176.2 1.3 slice_maximum_fusion.20
  177.5 1.2 slice_maximum_fusion.19
  181.0 1.2 slice_maximum_fusion.16
  182.2 1.3 slice_maximum_fusion.15
  183.6 1.3 slice_maximum_fusion.14
  187.2 1.2 slice_maximum_fusion.11
  188.4 1.2 slice_maximum_fusion.10
  189.6 1.2 slice_maximum_fusion.9
  192.0 1.2 slice_maximum_fusion.7
  193.2 1.4 slice_maximum_fusion.6
  194.6 1.2 slice_maximum_fusion.5
  195.8 1.2 slice_maximum_fusion.4
  200.1 1.2 copy.248
  201.5 1.2 copy.245
  202.9 1.2 copy.246
  204.2 1.2 copy.247
  205.6 1.2 copy.249
  209.0 1.2 copy.250
  210.9 1.2 copy.239
  212.9 1.2 copy.240
  223.4 1.2 copy.235
  238.0 1.2 copy.225
  239.9 1.2 copy.226
  241.9 1.2 copy.256
  351.6 11.4 stack.44
  365.9 1.8 fusion.3
  367.7 2.1 fusion.6
  369.8 1.7 convolution_bitcast_fusion.1
  373.2 940.1 %all-gather.5.cloned.1.call-done = f32[196608,128]{1,0:T(8,128)} async-done(((f32[384,128]{1,0:T(8,128)}), f32[196608,128]{1,0:T(8,128)}) %all-gather.5.cloned.1.call-update) | async-done | bytes 100663312 | tf_op jit(solution)/shard_map/all_gather | solution.py:151
  1313.3 30.9 %reduce_sum.9 = f32[384,128]{1,0:T(8,128)S(1)} reduce(f32[512,384,128]{2,1,0:T(8,128)} %bitcast.22, f32[]{:T(128)} %constant.82.clone.1), dimensions={0}, to_apply=%region_0.1 | reduce | flops 25116672 | bytes 100859904 | tf_op jit(solution)/shard_map/reduce_sum | solution.py:151
  (545 shorter events, 162.8 us)
Async XLA Ops:
  7.2 355.8 %copy-start = (bf16[125,128]{1,0:T(8,128)(2,1)S(1)}, bf16[125,128]{1,0:T(8,128)(2,1)}, u32[]{:S(2)}) copy-start(bf16[125,128]{1,0:T(8,128)(2,1)} %param.13) | copy-start | bytes 96004
  7.2 1306.1 %all-gather.5.cloned.1.call-start = ((), (), s32[]{:S(2)}) async-start(), calls=%async_computation | async-start | bytes 100859904 | tf_op jit(solution)/shard_map/all_gather | solution.py:151
  7.2 69.8 %collective-permute-start = (bf16[12,512]{1,0:T(8,128)(2,1)}, bf16[12,512]{1,0:T(8,128)(2,1)S(1)}, u32[]{:S(2)}, u32[]{:S(2)}) collective-permute-start(bf16[12,512]{1,0:T(8,128)(2,1)} %param.8), channel_id=1, source_target_pairs={{0,32},{32,64},{64,96},{96,128},{128,160},{160,192},{192,224},{224... | collective-permute-start | bytes 36872 | tf_op jit(solution)/shard_map/ppermute | solution.py:16
  11.3 65.8 %collective-permute-start.1 = (bf16[12,512]{1,0:T(8,128)(2,1)}, bf16[12,512]{1,0:T(8,128)(2,1)S(1)}, u32[]{:S(2)}, u32[]{:S(2)}) collective-permute-start(bf16[12,512]{1,0:T(8,128)(2,1)} %param.8), channel_id=1, source_target_pairs={{32,0},{64,32},{96,64},{128,96},{160,128},{192,160},{224,192},{256... | collective-permute-start | bytes 36872 | tf_op jit(solution)/shard_map/ppermute | solution.py:16
  77.8 9.4 collective-permute-start.3
  79.9 7.3 collective-permute-start.2
  112.8 51.1 %copy-start.118 = (s32[1,2]{1,0:T(1,128)S(1)}, s32[1,2]{1,0:T(1,128)}, u32[]{:S(2)}) copy-start(s32[1,2]{1,0:T(1,128)} %param.12) | copy-start | bytes 28
  208.2 14.1 %copy-start.65 = (bf16[8,8,8,8]{0,3,2,1:T(8,128)(2,1)S(1)}, bf16[8,8,8,8]{0,3,2,1:T(8,128)(2,1)}, u32[]{:S(2)}) copy-start(bf16[8,8,8,8]{0,3,2,1:T(8,128)(2,1)} %get-tuple-element.116) | copy-start | bytes 24580
  218.3 14.3 %copy-start.61 = (bf16[8,8,8,8]{0,3,2,1:T(8,128)(2,1)S(1)}, bf16[8,8,8,8]{0,3,2,1:T(8,128)(2,1)}, u32[]{:S(2)}) copy-start(bf16[8,8,8,8]{0,3,2,1:T(8,128)(2,1)} %get-tuple-element.107) | copy-start | bytes 24580
  219.4 14.3 %copy-start.60 = (bf16[8,8,8,8]{0,3,2,1:T(8,128)(2,1)S(1)}, bf16[8,8,8,8]{0,3,2,1:T(8,128)(2,1)}, u32[]{:S(2)}) copy-start(bf16[8,8,8,8]{0,3,2,1:T(8,128)(2,1)} %get-tuple-element.108) | copy-start | bytes 24580
  220.5 14.3 %copy-start.59 = (bf16[8,8,8,8]{0,3,2,1:T(8,128)(2,1)S(1)}, bf16[8,8,8,8]{0,3,2,1:T(8,128)(2,1)}, u32[]{:S(2)}) copy-start(bf16[8,8,8,8]{0,3,2,1:T(8,128)(2,1)} %get-tuple-element.109) | copy-start | bytes 24580
  221.5 14.3 %copy-start.58 = (bf16[8,8,8,8]{0,3,2,1:T(8,128)(2,1)S(1)}, bf16[8,8,8,8]{0,3,2,1:T(8,128)(2,1)}, u32[]{:S(2)}) copy-start(bf16[8,8,8,8]{0,3,2,1:T(8,128)(2,1)} %get-tuple-element.102) | copy-start | bytes 24580
  222.6 14.3 %copy-start.57 = (bf16[8,8,8,8]{0,3,2,1:T(8,128)(2,1)S(1)}, bf16[8,8,8,8]{0,3,2,1:T(8,128)(2,1)}, u32[]{:S(2)}) copy-start(bf16[8,8,8,8]{0,3,2,1:T(8,128)(2,1)} %get-tuple-element.103) | copy-start | bytes 24580
  229.5 14.3 %copy-start.56 = (bf16[8,8,8,8]{0,3,2,1:T(8,128)(2,1)S(1)}, bf16[8,8,8,8]{0,3,2,1:T(8,128)(2,1)}, u32[]{:S(2)}) copy-start(bf16[8,8,8,8]{0,3,2,1:T(8,128)(2,1)} %get-tuple-element.99) | copy-start | bytes 24580
  230.6 14.3 %copy-start.55 = (bf16[8,8,8,8]{0,3,2,1:T(8,128)(2,1)S(1)}, bf16[8,8,8,8]{0,3,2,1:T(8,128)(2,1)}, u32[]{:S(2)}) copy-start(bf16[8,8,8,8]{0,3,2,1:T(8,128)(2,1)} %get-tuple-element.100) | copy-start | bytes 24580
  236.1 14.1 %copy-start.50 = (bf16[8,8,8,8]{0,3,2,1:T(8,128)(2,1)S(1)}, bf16[8,8,8,8]{0,3,2,1:T(8,128)(2,1)}, u32[]{:S(2)}) copy-start(bf16[8,8,8,8]{0,3,2,1:T(8,128)(2,1)} %get-tuple-element.97) | copy-start | bytes 24580
  247.3 14.1 %copy-start.45 = (bf16[8,8,8,8]{0,3,2,1:T(8,128)(2,1)S(1)}, bf16[8,8,8,8]{0,3,2,1:T(8,128)(2,1)}, u32[]{:S(2)}) copy-start(bf16[8,8,8,8]{0,3,2,1:T(8,128)(2,1)} %get-tuple-element.89) | copy-start | bytes 24580
  258.5 14.1 %copy-start.40 = (bf16[8,8,8,8]{0,3,2,1:T(8,128)(2,1)S(1)}, bf16[8,8,8,8]{0,3,2,1:T(8,128)(2,1)}, u32[]{:S(2)}) copy-start(bf16[8,8,8,8]{0,3,2,1:T(8,128)(2,1)} %get-tuple-element.81) | copy-start | bytes 24580
  259.6 14.1 %copy-start.39 = (bf16[8,8,8,8]{0,3,2,1:T(8,128)(2,1)S(1)}, bf16[8,8,8,8]{0,3,2,1:T(8,128)(2,1)}, u32[]{:S(2)}) copy-start(bf16[8,8,8,8]{0,3,2,1:T(8,128)(2,1)} %get-tuple-element.74) | copy-start | bytes 24580
  260.7 14.1 %copy-start.38 = (bf16[8,8,8,8]{0,3,2,1:T(8,128)(2,1)S(1)}, bf16[8,8,8,8]{0,3,2,1:T(8,128)(2,1)}, u32[]{:S(2)}) copy-start(bf16[8,8,8,8]{0,3,2,1:T(8,128)(2,1)} %get-tuple-element.75) | copy-start | bytes 24580
  261.7 14.1 %copy-start.37 = (bf16[8,8,8,8]{0,3,2,1:T(8,128)(2,1)S(1)}, bf16[8,8,8,8]{0,3,2,1:T(8,128)(2,1)}, u32[]{:S(2)}) copy-start(bf16[8,8,8,8]{0,3,2,1:T(8,128)(2,1)} %get-tuple-element.76) | copy-start | bytes 24580
  262.8 14.5 %copy-start.36 = (bf16[8,8,8,8]{0,3,2,1:T(8,128)(2,1)S(1)}, bf16[8,8,8,8]{0,3,2,1:T(8,128)(2,1)}, u32[]{:S(2)}) copy-start(bf16[8,8,8,8]{0,3,2,1:T(8,128)(2,1)} %get-tuple-element.77) | copy-start | bytes 24580
  263.9 14.5 %copy-start.35 = (bf16[8,8,8,8]{0,3,2,1:T(8,128)(2,1)S(1)}, bf16[8,8,8,8]{0,3,2,1:T(8,128)(2,1)}, u32[]{:S(2)}) copy-start(bf16[8,8,8,8]{0,3,2,1:T(8,128)(2,1)} %get-tuple-element.70) | copy-start | bytes 24580
  264.9 14.5 %copy-start.34 = (bf16[8,8,8,8]{0,3,2,1:T(8,128)(2,1)S(1)}, bf16[8,8,8,8]{0,3,2,1:T(8,128)(2,1)}, u32[]{:S(2)}) copy-start(bf16[8,8,8,8]{0,3,2,1:T(8,128)(2,1)} %get-tuple-element.71) | copy-start | bytes 24580
  266.0 14.5 %copy-start.33 = (bf16[8,8,8,8]{0,3,2,1:T(8,128)(2,1)S(1)}, bf16[8,8,8,8]{0,3,2,1:T(8,128)(2,1)}, u32[]{:S(2)}) copy-start(bf16[8,8,8,8]{0,3,2,1:T(8,128)(2,1)} %get-tuple-element.72) | copy-start | bytes 24580
  272.9 14.5 %copy-start.32 = (bf16[8,8,8,8]{0,3,2,1:T(8,128)(2,1)S(1)}, bf16[8,8,8,8]{0,3,2,1:T(8,128)(2,1)}, u32[]{:S(2)}) copy-start(bf16[8,8,8,8]{0,3,2,1:T(8,128)(2,1)} %get-tuple-element.68) | copy-start | bytes 24580
  274.0 14.5 %copy-start.31 = (bf16[8,8,8,8]{0,3,2,1:T(8,128)(2,1)S(1)}, bf16[8,8,8,8]{0,3,2,1:T(8,128)(2,1)}, u32[]{:S(2)}) copy-start(bf16[8,8,8,8]{0,3,2,1:T(8,128)(2,1)} %get-tuple-element.69) | copy-start | bytes 24580
  275.1 14.5 %copy-start.30 = (bf16[8,8,8,8]{0,3,2,1:T(8,128)(2,1)S(1)}, bf16[8,8,8,8]{0,3,2,1:T(8,128)(2,1)}, u32[]{:S(2)}) copy-start(bf16[8,8,8,8]{0,3,2,1:T(8,128)(2,1)} %get-tuple-element.62) | copy-start | bytes 24580
  276.1 14.5 %copy-start.29 = (bf16[8,8,8,8]{0,3,2,1:T(8,128)(2,1)S(1)}, bf16[8,8,8,8]{0,3,2,1:T(8,128)(2,1)}, u32[]{:S(2)}) copy-start(bf16[8,8,8,8]{0,3,2,1:T(8,128)(2,1)} %get-tuple-element.63) | copy-start | bytes 24580
  277.6 14.1 %copy-start.28 = (bf16[8,8,8,8]{0,3,2,1:T(8,128)(2,1)S(1)}, bf16[8,8,8,8]{0,3,2,1:T(8,128)(2,1)}, u32[]{:S(2)}) copy-start(bf16[8,8,8,8]{0,3,2,1:T(8,128)(2,1)} %get-tuple-element.64) | copy-start | bytes 24580
  279.7 14.1 %copy-start.26 = (bf16[8,8,8,8]{0,3,2,1:T(8,128)(2,1)S(1)}, bf16[8,8,8,8]{0,3,2,1:T(8,128)(2,1)}, u32[]{:S(2)}) copy-start(bf16[8,8,8,8]{0,3,2,1:T(8,128)(2,1)} %get-tuple-element.58) | copy-start | bytes 24580
  287.7 14.1 %copy-start.24 = (bf16[8,8,8,8]{0,3,2,1:T(8,128)(2,1)S(1)}, bf16[8,8,8,8]{0,3,2,1:T(8,128)(2,1)}, u32[]{:S(2)}) copy-start(bf16[8,8,8,8]{0,3,2,1:T(8,128)(2,1)} %get-tuple-element.55) | copy-start | bytes 24580
  288.8 14.1 %copy-start.23 = (bf16[8,8,8,8]{0,3,2,1:T(8,128)(2,1)S(1)}, bf16[8,8,8,8]{0,3,2,1:T(8,128)(2,1)}, u32[]{:S(2)}) copy-start(bf16[8,8,8,8]{0,3,2,1:T(8,128)(2,1)} %get-tuple-element.56) | copy-start | bytes 24580
  289.8 14.1 %copy-start.22 = (bf16[8,8,8,8]{0,3,2,1:T(8,128)(2,1)S(1)}, bf16[8,8,8,8]{0,3,2,1:T(8,128)(2,1)}, u32[]{:S(2)}) copy-start(bf16[8,8,8,8]{0,3,2,1:T(8,128)(2,1)} %get-tuple-element.57) | copy-start | bytes 24580
  290.9 14.1 %copy-start.21 = (bf16[8,8,8,8]{0,3,2,1:T(8,128)(2,1)S(1)}, bf16[8,8,8,8]{0,3,2,1:T(8,128)(2,1)}, u32[]{:S(2)}) copy-start(bf16[8,8,8,8]{0,3,2,1:T(8,128)(2,1)} %get-tuple-element.50) | copy-start | bytes 24580
  292.0 14.1 %copy-start.20 = (bf16[8,8,8,8]{0,3,2,1:T(8,128)(2,1)S(1)}, bf16[8,8,8,8]{0,3,2,1:T(8,128)(2,1)}, u32[]{:S(2)}) copy-start(bf16[8,8,8,8]{0,3,2,1:T(8,128)(2,1)} %get-tuple-element.51) | copy-start | bytes 24580
  293.0 14.1 %copy-start.19 = (bf16[8,8,8,8]{0,3,2,1:T(8,128)(2,1)S(1)}, bf16[8,8,8,8]{0,3,2,1:T(8,128)(2,1)}, u32[]{:S(2)}) copy-start(bf16[8,8,8,8]{0,3,2,1:T(8,128)(2,1)} %get-tuple-element.52) | copy-start | bytes 24580
  294.1 14.1 %copy-start.18 = (bf16[8,8,8,8]{0,3,2,1:T(8,128)(2,1)S(1)}, bf16[8,8,8,8]{0,3,2,1:T(8,128)(2,1)}, u32[]{:S(2)}) copy-start(bf16[8,8,8,8]{0,3,2,1:T(8,128)(2,1)} %get-tuple-element.53) | copy-start | bytes 24580
  295.2 14.1 %copy-start.17 = (bf16[8,8,8,8]{0,3,2,1:T(8,128)(2,1)S(1)}, bf16[8,8,8,8]{0,3,2,1:T(8,128)(2,1)}, u32[]{:S(2)}) copy-start(bf16[8,8,8,8]{0,3,2,1:T(8,128)(2,1)} %get-tuple-element.46) | copy-start | bytes 24580
  308.5 14.3 %copy-start.10 = (bf16[8,8,8,8]{0,3,2,1:T(8,128)(2,1)S(1)}, bf16[8,8,8,8]{0,3,2,1:T(8,128)(2,1)}, u32[]{:S(2)}) copy-start(bf16[8,8,8,8]{0,3,2,1:T(8,128)(2,1)} %get-tuple-element.40) | copy-start | bytes 24580
  309.6 14.3 %copy-start.9 = (bf16[8,8,8,8]{0,3,2,1:T(8,128)(2,1)S(1)}, bf16[8,8,8,8]{0,3,2,1:T(8,128)(2,1)}, u32[]{:S(2)}) copy-start(bf16[8,8,8,8]{0,3,2,1:T(8,128)(2,1)} %get-tuple-element.41) | copy-start | bytes 24580
  317.6 15.2 %copy-start.8 = (bf16[8,8,8,8]{0,3,2,1:T(8,128)(2,1)S(1)}, bf16[8,8,8,8]{0,3,2,1:T(8,128)(2,1)}, u32[]{:S(2)}) copy-start(bf16[8,8,8,8]{0,3,2,1:T(8,128)(2,1)} %get-tuple-element.30) | copy-start | bytes 24580
  318.6 15.2 %copy-start.7 = (bf16[8,8,8,8]{0,3,2,1:T(8,128)(2,1)S(1)}, bf16[8,8,8,8]{0,3,2,1:T(8,128)(2,1)}, u32[]{:S(2)}) copy-start(bf16[8,8,8,8]{0,3,2,1:T(8,128)(2,1)} %get-tuple-element.31) | copy-start | bytes 24580
  319.7 15.2 %copy-start.6 = (bf16[8,8,8,8]{0,3,2,1:T(8,128)(2,1)S(1)}, bf16[8,8,8,8]{0,3,2,1:T(8,128)(2,1)}, u32[]{:S(2)}) copy-start(bf16[8,8,8,8]{0,3,2,1:T(8,128)(2,1)} %get-tuple-element.32) | copy-start | bytes 24580
  320.8 15.1 %copy-start.5 = (bf16[8,8,8,8]{0,3,2,1:T(8,128)(2,1)S(1)}, bf16[8,8,8,8]{0,3,2,1:T(8,128)(2,1)}, u32[]{:S(2)}) copy-start(bf16[8,8,8,8]{0,3,2,1:T(8,128)(2,1)} %get-tuple-element.33) | copy-start | bytes 24580
  322.0 15.0 %copy-start.4 = (bf16[8,8,8,8]{0,3,2,1:T(8,128)(2,1)S(1)}, bf16[8,8,8,8]{0,3,2,1:T(8,128)(2,1)}, u32[]{:S(2)}) copy-start(bf16[8,8,8,8]{0,3,2,1:T(8,128)(2,1)} %get-tuple-element.26) | copy-start | bytes 24580
  323.1 15.0 %copy-start.3 = (bf16[8,8,8,8]{0,3,2,1:T(8,128)(2,1)S(1)}, bf16[8,8,8,8]{0,3,2,1:T(8,128)(2,1)}, u32[]{:S(2)}) copy-start(bf16[8,8,8,8]{0,3,2,1:T(8,128)(2,1)} %get-tuple-element.27) | copy-start | bytes 24580
  324.1 14.9 %copy-start.2 = (bf16[8,8,8,8]{0,3,2,1:T(8,128)(2,1)S(1)}, bf16[8,8,8,8]{0,3,2,1:T(8,128)(2,1)}, u32[]{:S(2)}) copy-start(bf16[8,8,8,8]{0,3,2,1:T(8,128)(2,1)} %get-tuple-element.28) | copy-start | bytes 24580
  (78 other events, 663.1 us)
Sparse Core Ops, SparseCore 0:
  372.7 940.5 all-gather.4
